TPU v7x, 32 devices: a whole 2x2x4 slice. The times are simulated.
32 devices in a mesh: seq: 8 (over z, y), chan: 4 (over x, core).
Axes of the slice: x: 2, y: 2, z: 4, core: 2. Of those that a mesh axis runs over, the one named last changes fastest.
Arguments:
- output_gate: bfloat16 [256, 16384], P('chan', 'seq'), may hold values from -6 to 6
- input_gate: bfloat16 [256, 16384], P('chan', 'seq'), may hold values from -6 to 6
- signal: bfloat16 [256, 16384], P('chan', 'seq'), may hold values from -6 to 6
- cotangent: bfloat16 [256, 16384], P('chan', 'seq'), may hold values from -6 to 6
- long_filter: float32 [64, 16384], P(None, 'seq'), may hold values from -1 to 1
Outputs:
- grad_output_gate: bfloat16 [256, 16384], P('chan', 'seq')
- grad_input_gate: bfloat16 [256, 16384], P('chan', 'seq')
- grad_signal: bfloat16 [256, 16384], P('chan', 'seq')
- grad_filter: float32 [64, 16384], P('chan', 'seq')
All inputs are finite; a program needn't handle non-finite values.
Results may differ from a plain program's by a relative error of at most 0.0022.
Values sent between devices are 32-bit elements; how exact they have to be, the bound alone decides.
A program may use at most 128 MiB of HBM per device.

v0:
```python
import math

import jax
import jax.numpy as jnp
from jax import lax
from jax.sharding import PartitionSpec as P

ROW = 512


def trig_table(first, second, modulus):
    product = first[:, None] * second[None, :] % modulus
    angle = product.astype(jnp.float32) * (2.0 * math.pi / modulus)
    return (jnp.cos(angle), jnp.sin(angle))


def contract(form, left, right):
    return jnp.einsum(
        form, left, right, precision=lax.Precision.HIGHEST, preferred_element_type=jnp.float32
    )


def per_device(output_gate, input_gate, signal, cotangent, long_filter):
    seq_count = lax.axis_size("seq")
    seq_place = lax.axis_index("seq")
    channels, tok_local = signal.shape
    rows_dev = tok_local // ROW
    factor = 2 * rows_dev * seq_count
    cols_dev = ROW // seq_count
    freq_dev = factor // seq_count
    length = factor * ROW
    row_iota = jnp.arange(ROW, dtype=jnp.int32)
    factor_iota = jnp.arange(factor, dtype=jnp.int32)
    half_iota = jnp.arange(factor // 2, dtype=jnp.int32)
    row_cos, row_sin = trig_table(row_iota, row_iota, ROW)
    first_cos, first_sin = trig_table(half_iota, factor_iota, factor)
    col_start = seq_place * cols_dev + jnp.arange(cols_dev, dtype=jnp.int32)
    twist_cos, twist_sin = trig_table(col_start, factor_iota, length)
    freq_start = seq_place * freq_dev + jnp.arange(freq_dev, dtype=jnp.int32)
    back_cos, back_sin = trig_table(freq_start, row_iota, length)
    mixed = input_gate.astype(jnp.float32) * signal.astype(jnp.float32)
    gated = cotangent.astype(jnp.float32) * output_gate.astype(jnp.float32)
    stacked = jnp.concatenate([mixed, gated, long_filter], axis=0)
    members = stacked.shape[0]
    blocks = stacked.reshape(members, rows_dev, ROW)
    pieces = lax.all_to_all(blocks, "seq", split_axis=2, concat_axis=1, tiled=True)
    real_part = contract("cak,ab->ckb", pieces, first_cos)
    imag_part = -contract("cak,ab->ckb", pieces, first_sin)
    twisted = jnp.stack(
        [
            real_part * twist_cos + imag_part * twist_sin,
            imag_part * twist_cos - real_part * twist_sin,
        ]
    )
    pieces = lax.all_to_all(twisted, "seq", split_axis=3, concat_axis=2, tiled=True)
    real_in = pieces[0]
    imag_in = pieces[1]
    spec_real = contract("ctj,tm->cjm", real_in, row_cos) + contract(
        "ctj,tm->cjm", imag_in, row_sin
    )
    spec_imag = contract("ctj,tm->cjm", imag_in, row_cos) - contract(
        "ctj,tm->cjm", real_in, row_sin
    )
    spec_real, spec_imag = (spec_real, spec_imag)
    filter_real = spec_real[2 * channels :]
    filter_imag = spec_imag[2 * channels :]
    mixed_real = spec_real[:channels]
    mixed_imag = spec_imag[:channels]
    gated_real = spec_real[channels : 2 * channels]
    gated_imag = spec_imag[channels : 2 * channels]
    response_real = filter_real * mixed_real - filter_imag * mixed_imag
    response_imag = filter_real * mixed_imag + filter_imag * mixed_real
    back_real = filter_real * gated_real + filter_imag * gated_imag
    back_imag = filter_real * gated_imag - filter_imag * gated_real
    kernel_real = mixed_real * gated_real + mixed_imag * gated_imag
    kernel_imag = mixed_real * gated_imag - mixed_imag * gated_real
    real_in = jnp.concatenate([response_real, back_real, kernel_real], axis=0)
    imag_in = jnp.concatenate([response_imag, back_imag, kernel_imag], axis=0)
    turn_real = contract("cjm,mt->cjt", real_in, row_cos) - contract(
        "cjm,mt->cjt", imag_in, row_sin
    )
    turn_imag = contract("cjm,mt->cjt", imag_in, row_cos) + contract(
        "cjm,mt->cjt", real_in, row_sin
    )
    stacked = jnp.stack(
        [turn_real * back_cos - turn_imag * back_sin, turn_imag * back_cos + turn_real * back_sin]
    )
    pieces = lax.all_to_all(stacked, "seq", split_axis=3, concat_axis=2, tiled=True)
    real_part = contract("ckj,ak->caj", pieces[0], first_cos) - contract(
        "ckj,ak->caj", pieces[1], first_sin
    )
    columns = real_part / length
    row_blocks = lax.all_to_all(columns, "seq", split_axis=1, concat_axis=2, tiled=True)
    results = row_blocks.reshape(row_blocks.shape[0], tok_local)
    kernel = lax.psum_scatter(results[2 * channels :], "chan", scatter_dimension=0, tiled=True)
    response = results[:channels]
    grad_mixed = results[channels : 2 * channels]
    grad_filter = kernel / math.sqrt(tok_local * seq_count)
    grad_output_gate = (cotangent.astype(jnp.float32) * response).astype(jnp.bfloat16)
    grad_input_gate = (grad_mixed * signal.astype(jnp.float32)).astype(jnp.bfloat16)
    grad_signal = (grad_mixed * input_gate.astype(jnp.float32)).astype(jnp.bfloat16)
    return (grad_output_gate, grad_input_gate, grad_signal, grad_filter)


def solution(mesh):
    placed = (
        P("chan", "seq"),
        P("chan", "seq"),
        P("chan", "seq"),
        P("chan", "seq"),
        P(None, "seq"),
    )
    return jax.shard_map(
        per_device,
        mesh=mesh,
        in_specs=placed,
        out_specs=(P("chan", "seq"), P("chan", "seq"), P("chan", "seq"), P("chan", "seq")),
        check_vma=False,
    )
```

profile of v0, /device:TPU:0, one launch (start us, length us, event | category | flops | bytes accessed | tf_op | source)
XLA Modules:
  0.0 693.2 jit_solution(13572251819304777482)
XLA Ops:
  13.2 7.3 %all-to-all-start = ((f32[192,4,512]{0,1,2:T(4,128)}), f32[192,4,512]{0,1,2:T(4,128)S(1)}, u32[]{:S(2)}, u32[]{:S(2)}) async-start(f32[192,4,512]{0,1,2:T(4,128)} %copy.62), calls=%async_computation | async-start | bytes 4194304 | tf_op jit(solution)/shard_map/all_to_all | solution.py:46
  20.7 48.0 %all-to-all-done = f32[192,4,512]{0,1,2:T(4,128)S(1)} async-done(((f32[192,4,512]{0,1,2:T(4,128)}), f32[192,4,512]{0,1,2:T(4,128)S(1)}, u32[]{:S(2)}, u32[]{:S(2)}) %all-to-all-start) | async-done | bytes 1572896 | tf_op jit(solution)/shard_map/all_to_all | solution.py:46
  77.6 5.8 add_bitcast_fusion
  84.7 8.5 %copy.65 = f32[2,192,64,64]{1,2,0,3:T(8,128)} copy(f32[2,192,64,64]{1,3,2,0:T(8,128)S(1)} %pad_maximum_fusion) | data formatting | bytes 12582912 | tf_op jit(solution)/shard_map/stack | solution.py:49
  93.2 5.0 all-to-all-start.1
  98.4 182.0 %all-to-all-done.1 = f32[2,192,64,64]{1,2,0,3:T(8,128)} async-done(((f32[2,192,64,64]{1,2,0,3:T(8,128)}), f32[2,192,64,64]{1,2,0,3:T(8,128)}, u32[]{:S(2)}, u32[]{:S(2)}) %all-to-all-start.1) | async-done | bytes 6291488 | tf_op jit(solution)/shard_map/all_to_all | solution.py:55
  280.4 9.9 %copy.90 = f32[2,192,64,8,8]{1,4,2,3,0:T(8,128)S(1)} copy(f32[2,192,64,8,8]{1,2,0,4,3:T(8,128)} %bitcast.6) | data formatting | bytes 12582912 | tf_op jit(solution)/shard_map/all_to_all | solution.py:55
  294.1 4.3 copy.67
  298.4 10.5 %fusion.25 = f32[192,8,512]{2,1,0:T(8,128)} fusion(f32[192,512,8]{1,2,0:T(8,128)S(1)} %copy.67), kind=kOutput, calls=%fused_computation.39 | convolution fusion | flops 4835508224 | bytes 6291456 | tf_op jit(solution)/shard_map/ctj,tm->cjm/dot_general | solution.py:18
  308.9 5.4 copy.68
  314.3 13.4 %fusion.23 = f32[192,8,512]{2,1,0:T(8,128)S(1)} fusion(f32[192,512,8]{1,2,0:T(8,128)} %copy.68), kind=kOutput, calls=%fused_computation.37 | convolution fusion | flops 4835508224 | bytes 6291456 | tf_op jit(solution)/shard_map/ctj,tm->cjm/dot_general | solution.py:18
  327.7 11.7 %convolution_add_fusion = f32[192,8,512]{2,1,0:T(8,128)S(1)} fusion(f32[192,8,512]{2,1,0:T(8,128)S(1)} %copy-done.1, f32[192,512,8]{1,2,0:T(8,128)S(1)} %copy-done), kind=kOutput, calls=%fused_computation.23 | convolution fusion | flops 4836294656 | bytes 9437184 | tf_op jit(solution)/shard_map/ctj,tm->cjm/dot_general | solution.py:18
  339.4 11.9 %convolution_subtract_fusion = f32[192,8,512]{2,1,0:T(8,128)S(1)} fusion(f32[192,8,512]{2,1,0:T(8,128)S(1)} %fusion.23, f32[192,512,8]{1,2,0:T(8,128)S(1)} %copy.67), kind=kOutput, calls=%fused_computation.22 | convolution fusion | flops 4836294656 | bytes 9437184 | tf_op jit(solution)/shard_map/ctj,tm->cjm/dot_general | solution.py:18
  352.9 9.2 %fusion.6 = f32[192,8,512]{2,1,0:T(8,128)S(1)} fusion(f32[64,8,512]{2,1,0:T(8,128)S(1)} %get-tuple-element.15, f32[64,8,512]{2,1,0:T(8,128)S(1)} %get-tuple-element.14, f32[64,8,512]{2,1,0:T(8,128)S(1)} %get-tuple-element.17), kind=kOutput, calls=%fused_computation.15 | convolution fusion | flops 4837081088 | bytes 6291456 | tf_op jit(solution)/shard_map/cjm,mt->cjt/dot_general | solution.py:18
  362.1 9.2 %fusion.7 = f32[192,8,512]{2,1,0:T(8,128)S(1)} fusion(f32[64,8,512]{2,1,0:T(8,128)S(1)} %get-tuple-element.15, f32[64,8,512]{2,1,0:T(8,128)S(1)} %get-tuple-element.14, f32[64,8,512]{2,1,0:T(8,128)S(1)} %get-tuple-element.17), kind=kOutput, calls=%fused_computation.16 | convolution fusion | flops 4837081088 | bytes 6291456 | tf_op jit(solution)/shard_map/cjm,mt->cjt/dot_general | solution.py:18
  371.3 9.7 %fusion.10 = f32[192,8,512]{2,1,0:T(8,128)S(1)} fusion(f32[192,8,512]{2,1,0:T(8,128)S(1)} %fusion.7, f32[64,8,512]{2,1,0:T(8,128)S(1)} %get-tuple-element.13, f32[64,8,512]{2,1,0:T(8,128)S(1)} %get-tuple-element.16, f32[64,8,512]{2,1,0:T(8,128)S(1)} %get-tuple-element.12), kind=kOutput, calls=%fused_computation.20 | convolution fusion | flops 4837867520 | bytes 9437184 | tf_op jit(solution)/shard_map/cjm,mt->cjt/dot_general | solution.py:18
  380.9 10.1 %subtract_bitcast_fusion.1 = (f32[1,192,8,512]{3,2,1,0:T(8,128)S(1)}, f32[1,192,8,512]{3,2,1,0:T(8,128)S(1)}) fusion(f32[192,8,512]{2,1,0:T(8,128)S(1)} %fusion.10, f32[8,512]{1,0:T(8,128)S(1)} %get-tuple-element.24, f32[8,512]{1,0:T(8,128)S(1)} %get-tuple-element.23, f32[192,8,512]{2,1,0:T(8,128)S(1)} %fusion.6, f32[64,8,512]{2,1,0:T(8,128)S(1)} %get-tuple-element.13, ...), kind=kOutput, calls=%fused_computation.14 | convolution fusion | flops 4842586112 | bytes 15761408 | tf_op jit(solution)/shard_map/cjm,mt->cjt/dot_general | solution.py:18
  394.4 9.6 %copy.71 = f32[2,192,8,512]{1,2,0,3:T(8,128)} copy(f32[2,192,8,512]{3,2,1,0:T(8,128)} %pad_maximum_fusion.1) | data formatting | bytes 12582912 | tf_op jit(solution)/shard_map/stack | solution.py:85
  404.0 186.8 %all_to_all.63 = f32[2,192,8,512]{1,2,0,3:T(8,128)S(1)} all-to-all(f32[2,192,8,512]{1,2,0,3:T(8,128)} %copy.71), channel_id=1, replica_groups=mesh['seq'=8,'chan'=4] {'seq'}, dimensions={3} | all-to-all | bytes 12582912 | tf_op jit(solution)/shard_map/all_to_all | solution.py:88
  590.8 4.9 copy.72
  596.8 4.6 fusion
  601.4 5.0 multiply_bitcast_fusion
  607.6 51.4 %all_to_all.64 = f32[192,32,64]{0,2,1:T(8,128)S(1)} all-to-all(f32[192,32,64]{0,2,1:T(8,128)S(1)} %copy.75), channel_id=1, replica_groups=mesh['seq'=8,'chan'=4] {'seq'}, dimensions={1} | all-to-all | bytes 3145728 | tf_op jit(solution)/shard_map/all_to_all | solution.py:93
  668.1 16.5 %reduce-scatter.2.cloned.1.call-done = f32[16,2048]{1,0:T(8,128)} async-done(((f32[64,2048]{1,0:T(8,128)}), f32[16,2048]{1,0:T(8,128)}) %reduce-scatter.2.cloned.1.call-update) | async-done | bytes 131088 | tf_op jit(solution)/shard_map/reduce_scatter | solution.py:95
  (41 shorter events, 38.4 us)
Async XLA Ops:
  13.2 55.5 %all-to-all-start = ((f32[192,4,512]{0,1,2:T(4,128)}), f32[192,4,512]{0,1,2:T(4,128)S(1)}, u32[]{:S(2)}, u32[]{:S(2)}) async-start(f32[192,4,512]{0,1,2:T(4,128)} %copy.62), calls=%async_computation | async-start | bytes 4194304 | tf_op jit(solution)/shard_map/all_to_all | solution.py:46
  93.2 187.2 %all-to-all-start.1 = ((f32[2,192,64,64]{1,2,0,3:T(8,128)}), f32[2,192,64,64]{1,2,0,3:T(8,128)}, u32[]{:S(2)}, u32[]{:S(2)}) async-start(f32[2,192,64,64]{1,2,0,3:T(8,128)} %copy.65), calls=%async_computation.1 | async-start | bytes 16777216 | tf_op jit(solution)/shard_map/all_to_all | solution.py:55
  98.2 586.3 %reduce-scatter.2.cloned.1.call-start = ((), (), s32[]{:S(2)}) async-start(), calls=%async_computation.5 | async-start | bytes 655360 | tf_op jit(solution)/shard_map/reduce_scatter | solution.py:95
  314.3 13.4 %copy-start = (f32[192,512,8]{1,2,0:T(8,128)S(1)}, f32[192,512,8]{1,2,0:T(8,128)}, u32[]{:S(2)}) copy-start(f32[192,512,8]{1,2,0:T(8,128)} %copy.68) | copy-start | bytes 9437188
  314.3 13.4 %copy-start.1 = (f32[192,8,512]{2,1,0:T(8,128)S(1)}, f32[192,8,512]{2,1,0:T(8,128)}, u32[]{:S(2)}) copy-start(f32[192,8,512]{2,1,0:T(8,128)} %fusion.25) | copy-start | bytes 9437188
  664.7 1.7 copy-start.2
  664.8 2.4 copy-start.3
  664.8 2.4 copy-start.4
Sparse Core Ops, SparseCore 0:
  663.9 20.5 reduce-scatter.1
where the time goes:
time: 698 us; the launch traced here: 693 us
  waiting for transfers between devices  246 us (35%)
  blocking collectives  238 us (34%)
  matrix products  104 us (15%)
  local copies, waits for them, and re-layouts  64.9 us (9%)
  between operations  14.5 us (2%)
  other arithmetic  12.4 us (2%)
  starting transfers between devices  12.3 us (2%)
    all_to_all x1, blocking collectives, per_device(): lax.all_to_all(stacked, 'seq', split_axis=3, concat_axis=2, tiled=True)  187 us
    all_to_all x1, waiting for transfers between devices, per_device(): lax.all_to_all(twisted, 'seq', split_axis=3, concat_axis=2, tiled=True)  182 us
    dot_general x12, matrix products, contract(): jnp.einsum(form, left, right, precision=lax.Precision.HIGHEST, preferred_...  104 us
    all_to_all x1, blocking collectives, per_device(): lax.all_to_all(columns, 'seq', split_axis=1, concat_axis=2, tiled=True)  51.4 us
    all_to_all x1, waiting for transfers between devices, per_device(): lax.all_to_all(blocks, 'seq', split_axis=2, concat_axis=1, tiled=True)  48 us
    reduce_scatter x1, waiting for transfers between devices, per_device(): lax.psum_scatter(results[2 * channels:], 'chan', scatter_dimension=0, til...  16.5 us
  transfers between devices with their start and end apart: 3, of which 3 were waited for; matrix products, arithmetic and copies ran while one was open for 1% of the time, Pallas kernels for 0%

commit v1 on v0

v1 whole, which is shorter than its diff:
```python
import functools
import math

import jax
import jax.numpy as jnp
import numpy as np
from jax import lax
from jax.experimental import pallas as pl
from jax.experimental.pallas import tpu as pltpu
from jax.sharding import PartitionSpec as P


def split_bf16(value):
    high = value.astype(jnp.bfloat16)
    return high, (value - high.astype(jnp.float32)).astype(jnp.bfloat16)


def tables(rows, cols):
    total = rows * cols
    row = np.arange(rows)
    col = np.arange(cols)
    angle = 2.0 * np.pi * ((4 * row[:, None] + 1) * row[None, :] % (4 * rows)) / (4 * rows)
    first = np.concatenate([np.cos(angle), -np.sin(angle)], axis=0)
    angle = 2.0 * np.pi * (col[:, None] * col[None, :] % cols) / cols
    cos, sin = np.cos(angle), np.sin(angle)
    second = np.block([[cos, -sin], [sin, cos]])
    angle = 2.0 * np.pi * ((4 * row[:, None] + 1) * col[None, :]) / (4 * total)
    twist = np.stack([np.cos(angle), -np.sin(angle)]).astype(np.float32)
    out = []
    for table in (first, second, second.T, first.T / total):
        out += list(split_bf16(jnp.asarray(table.astype(np.float32))))
    return out + [jnp.asarray(twist)]


def product(left, right):
    dot = functools.partial(jnp.dot, preferred_element_type=jnp.float32)
    return dot(left[0], right[0]) + dot(left[0], right[1]) + dot(left[1], right[0])


def transform_kernel(
    repeat, rows, cols, kernel_scale,
    mixed_ref, gated_ref, filter_ref,
    first_hi, first_lo, second_hi, second_lo, back_hi, back_lo, last_hi, last_lo, twist_ref,
    response_ref, grad_ref, kernel_ref,
):
    first = (first_hi[...], first_lo[...])
    second = (second_hi[...], second_lo[...])
    back = (back_hi[...], back_lo[...])
    last = (last_hi[...], last_lo[...])
    twist_re = twist_ref[0]
    twist_im = twist_ref[1]

    def forward(block):
        part = product(first, split_bf16(block))
        re, im = part[:rows], part[rows:]
        turned = jnp.concatenate(
            [re * twist_re - im * twist_im, re * twist_im + im * twist_re], axis=1
        )
        spec = product(split_bf16(turned), second)
        return spec[:, :cols], spec[:, cols:]

    def inverse(re, im):
        part = product(split_bf16(jnp.concatenate([re, im], axis=1)), back)
        re, im = part[:, :cols], part[:, cols:]
        turned = jnp.concatenate(
            [re * twist_re + im * twist_im, im * twist_re - re * twist_im], axis=0
        )
        return product(last, split_bf16(turned))

    h_re, h_im = forward(filter_ref[0])
    k_re = k_im = 0.0
    for place in range(repeat):
        m_re, m_im = forward(mixed_ref[0, place])
        g_re, g_im = forward(gated_ref[0, place])
        response_ref[0, place] = inverse(h_re * m_re - h_im * m_im, h_re * m_im + h_im * m_re)
        grad_ref[0, place] = inverse(h_re * g_re + h_im * g_im, h_re * g_im - h_im * g_re)
        k_re += m_re * g_re + m_im * g_im
        k_im += m_re * g_im - m_im * g_re
    kernel_ref[0] = inverse(k_re, k_im) * kernel_scale


def transform(mixed, gated, filters):
    count, repeat, rows, cols = mixed.shape
    constants = tables(rows, cols)
    whole = [
        pl.BlockSpec(table.shape, lambda i, rank=table.ndim: (0,) * rank) for table in constants
    ]
    many = pl.BlockSpec((1, repeat, rows, cols), lambda i: (i, 0, 0, 0))
    one = pl.BlockSpec((1, rows, cols), lambda i: (i, 0, 0))
    total = rows * cols
    return pl.pallas_call(
        functools.partial(transform_kernel, repeat, rows, cols, 1.0 / math.sqrt(total)),
        grid=(count,),
        in_specs=[many, many, one] + whole,
        out_specs=[many, many, one],
        out_shape=[
            jax.ShapeDtypeStruct(mixed.shape, jnp.float32),
            jax.ShapeDtypeStruct(mixed.shape, jnp.float32),
            jax.ShapeDtypeStruct(filters.shape, jnp.float32),
        ],
        compiler_params=pltpu.CompilerParams(vmem_limit_bytes=48 * 1024 * 1024),
        name="transform",
    )(mixed, gated, filters, *constants)


def per_device(output_gate, input_gate, signal, cotangent, long_filter):
    seq_count = lax.axis_size("seq")
    chan_count = lax.axis_size("chan")
    channels, tok_local = signal.shape
    filters = long_filter.shape[0]
    tokens = tok_local * seq_count
    cols = 2 ** (int(math.log2(tokens)) // 2)
    rows = tokens // cols
    rows_dev = rows // seq_count
    spread = channels == filters and filters % (seq_count * chan_count) == 0
    repeat = chan_count if spread else 1
    axes = ("chan", "seq") if spread else ("seq",)
    parts = seq_count * repeat
    held = filters // parts

    mixed = input_gate.astype(jnp.float32) * signal.astype(jnp.float32)
    gated = cotangent.astype(jnp.float32) * output_gate.astype(jnp.float32)
    stacked = jnp.stack([mixed, gated], axis=0).reshape(2, parts, held, rows_dev, cols)
    pieces = lax.all_to_all(stacked.transpose(1, 0, 2, 3, 4), axes, 0, 0)
    pieces = pieces.reshape(repeat, seq_count, 2, held, rows_dev, cols)
    pieces = pieces.transpose(2, 3, 0, 1, 4, 5).reshape(2, held, repeat, rows, cols)
    if spread:
        span = held * seq_count
        long_filter = lax.dynamic_slice_in_dim(
            long_filter, lax.axis_index("chan") * span, span, axis=0
        )
    taps = long_filter.reshape(seq_count, held, rows_dev, cols)
    taps = lax.all_to_all(taps, "seq", 0, 0).transpose(1, 0, 2, 3).reshape(held, rows, cols)

    response, grad_mixed, kernel = transform(pieces[0], pieces[1], taps)

    kernel = kernel.reshape(held, seq_count, rows_dev, cols).transpose(1, 0, 2, 3)
    kernel = lax.all_to_all(kernel, "seq", 0, 0).reshape(held * seq_count, tok_local)
    if not spread:
        kernel = lax.psum_scatter(kernel, "chan", scatter_dimension=0, tiled=True)
    results = jnp.stack([response, grad_mixed]).reshape(
        2, held, repeat, seq_count, rows_dev, cols
    )
    results = results.transpose(2, 3, 0, 1, 4, 5).reshape(parts, 2, held, rows_dev, cols)
    results = lax.all_to_all(results, axes, 0, 0)
    results = results.transpose(1, 0, 2, 3, 4).reshape(2, channels, tok_local)
    response, grad_mixed = results[0], results[1]
    grad_output_gate = (cotangent.astype(jnp.float32) * response).astype(jnp.bfloat16)
    grad_input_gate = (grad_mixed * signal.astype(jnp.float32)).astype(jnp.bfloat16)
    grad_signal = (grad_mixed * input_gate.astype(jnp.float32)).astype(jnp.bfloat16)
    return (grad_output_gate, grad_input_gate, grad_signal, kernel)


def solution(mesh):
    placed = (
        P("chan", "seq"),
        P("chan", "seq"),
        P("chan", "seq"),
        P("chan", "seq"),
        P(None, "seq"),
    )
    return jax.shard_map(
        per_device,
        mesh=mesh,
        in_specs=placed,
        out_specs=(P("chan", "seq"), P("chan", "seq"), P("chan", "seq"), P("chan", "seq")),
        check_vma=False,
    )
```

time: 698 us -> 98.1 us (0.14)
  blocking collectives: 238 us -> 0 us
  waiting for transfers between devices: 246 us -> 65.4 us
  matrix products: 104 us -> 0 us
  local copies, waits for them, and re-layouts: 64.9 us -> 6.73 us
  between operations: 14.5 us -> 0.87 us
  other arithmetic: 12.4 us -> 2.5 us
    all_to_all x2 -> x0, blocking collectives: 238 us -> none  [the longest x1 187 us: per_device(): lax.all_to_all(stacked, 'seq', split_axis=3, concat_axis=2, tiled=True)]
    all_to_all x2 -> x4, waiting for transfers between devices: 230 us -> 65.4 us  [the longest x1 27.6 us: per_device(): pieces = lax.all_to_all(stacked.transpose(1, 0, 2, 3, 4), axes, 0, 0)]
    dot_general x12 -> x0, matrix products: 104 us -> none  [contract(): jnp.einsum(form, left, right, precision=lax.Precision.HIGHEST, preferred_...]
    all_to_all x5 -> x0, local copies, waits for them, and re-layouts: 20 us -> none  [the longest x1 9.87 us: per_device(): lax.all_to_all(twisted, 'seq', split_axis=3, concat_axis=2, tiled=True)]
    another operation x2 -> x0, local copies, waits for them, and re-layouts: 18.1 us -> none  [the longest x1 9.57 us: per_device(): jnp.stack([turn_real * back_cos - turn_imag * back_sin, turn_imag * back_...]
    reduce_scatter x1 -> x0, waiting for transfers between devices: 16.5 us -> none  [per_device(): lax.psum_scatter(results[2 * channels:], 'chan', scatter_dimension=0, til...]
    slice x9 -> x2, local copies, waits for them, and re-layouts: 12.3 us -> 0.17 us  [the longest x1 0.09 us: per_device(): response, grad_mixed, kernel = transform(pieces[0], pieces[1], taps)]
    squeeze x2 -> x0, local copies, waits for them, and re-layouts: 9.75 us -> none  [the longest x1 5.4 us: per_device(): imag_in = pieces[1]]
  transfers between devices with their start and end apart: 3 -> 4, of which waited for: 3 -> 4; matrix products, arithmetic and copies ran while one was open for 1% -> 3% of each run, Pallas kernels for 0% -> 0%
where the time goes in v1:
time: 98.1 us; the launch traced here: 97.5 us
  waiting for transfers between devices  65.4 us (67%)
  starting transfers between devices  15.9 us (16%)
  local copies, waits for them, and re-layouts  6.73 us (7%)
  Pallas kernels  6.1 us (6%)
  other arithmetic  2.5 us (3%)
    all_to_all x1, waiting for transfers between devices, per_device(): pieces = lax.all_to_all(stacked.transpose(1, 0, 2, 3, 4), axes, 0, 0)  27.6 us
    all_to_all x1, waiting for transfers between devices, per_device(): results = lax.all_to_all(results, axes, 0, 0)  26.9 us
    all_to_all x1, starting transfers between devices, per_device(): lax.all_to_all(taps, 'seq', 0, 0).transpose(1, 0, 2, 3)  7.28 us
    pallas_call x1, Pallas kernels, transform(): pl.pallas_call(functools.partial(transform_kernel, repeat, rows, cols, 1....  6.1 us
    all_to_all x1, waiting for transfers between devices, per_device(): lax.all_to_all(kernel, 'seq', 0, 0).reshape(held * seq_count, tok_local)  6.01 us
    all_to_all x1, waiting for transfers between devices, per_device(): lax.all_to_all(taps, 'seq', 0, 0).transpose(1, 0, 2, 3)  4.93 us
    unnamed x33, local copies, waits for them, and re-layouts  4.62 us
    all_to_all x1, starting transfers between devices, per_device(): lax.all_to_all(kernel, 'seq', 0, 0).reshape(held * seq_count, tok_local)  3.37 us
  transfers between devices with their start and end apart: 4, of which 4 were waited for; matrix products, arithmetic and copies ran while one was open for 3% of the time, Pallas kernels for 0%

profile of v1, /device:TPU:0, one launch (start us, length us, event | category | flops | bytes accessed | tf_op | source)
XLA Modules:
  0.0 97.5 jit_solution(15916592266168926118)
XLA Ops:
  0.6 1.0 %copy-done = f32[64,2048]{1,0:T(8,128)S(1)} copy-done((f32[64,2048]{1,0:T(8,128)S(1)}, f32[64,2048]{1,0:T(8,128)}, u32[]{:S(2)}) %copy-start) | copy-done | bytes 524312
  1.7 0.7 copy.27
  2.4 7.3 %all-to-all-start.1 = ((f32[8,2,16,128]{3,2,1,0:T(8,128)}), f32[8,2,16,128]{3,2,1,0:T(8,128)S(1)}, u32[]{:S(2)}, u32[]{:S(2)}) async-start(f32[8,2,16,128]{3,2,1,0:T(8,128)} %bitcast.24), calls=%async_computation.1 | async-start | bytes 262144 | tf_op jit(solution)/shard_map/all_to_all | solution.py:133
  9.8 0.9 copy-done.10
  10.6 0.1 copy-done.12
  10.8 0.1 copy.26
  10.9 0.1 copy.25
  11.0 1.1 %maximum_bitcast_fusion = f32[32,2,2,16,128]{4,3,2,1,0:T(8,128)} fusion(f32[1,32,2,16,128]{4,3,2,0,1:T(8,128)S(1)} %bitcast.61, f32[1,32,2,16,128]{4,3,2,0,1:T(8,128)S(1)} %bitcast.62), kind=kLoop, calls=%fused_computation | loop fusion | flops 262144 | bytes 2097152 | tf_op jit(solution)/shard_map/transpose | solution.py:124
  12.1 4.9 %all-to-all-done.1 = f32[8,2,16,128]{3,2,1,0:T(8,128)S(1)} async-done(((f32[8,2,16,128]{3,2,1,0:T(8,128)}), f32[8,2,16,128]{3,2,1,0:T(8,128)S(1)}, u32[]{:S(2)}, u32[]{:S(2)}) %all-to-all-start.1) | async-done | bytes 131104 | tf_op jit(solution)/shard_map/all_to_all | solution.py:133
  17.0 2.6 %all-to-all-start = ((f32[32,2,2,16,128]{4,3,2,1,0:T(8,128)}), f32[32,2,2,16,128]{4,3,2,1,0:T(8,128)S(1)}, u32[]{:S(2)}, u32[]{:S(2)}) async-start(f32[32,2,2,16,128]{4,3,2,1,0:T(8,128)} %maximum_bitcast_fusion), calls=%async_computation | async-start | bytes 2097152 | tf_op jit(solution)/shard_map/all_to_all | solution.py:124
  19.7 27.6 %all-to-all-done = f32[32,2,2,16,128]{4,3,2,1,0:T(8,128)S(1)} async-done(((f32[32,2,2,16,128]{4,3,2,1,0:T(8,128)}), f32[32,2,2,16,128]{4,3,2,1,0:T(8,128)S(1)}, u32[]{:S(2)}, u32[]{:S(2)}) %all-to-all-start) | async-done | bytes 1048608 | tf_op jit(solution)/shard_map/all_to_all | solution.py:124
  47.3 0.1 copy.37
  47.5 0.1 fusion.6
  47.6 0.7 copy-done.1
  48.6 6.1 %transform.1 = (f32[2,4,128,128]{3,2,1,0:T(8,128)S(1)}, f32[2,4,128,128]{3,2,1,0:T(8,128)S(1)}, f32[2,128,128]{2,1,0:T(8,128)S(1)}) custom-call(f32[2,4,128,128]{3,2,1,0:T(8,128)S(1)} %bitcast.51, f32[2,4,128,128]{3,2,1,0:T(8,128)S(1)} %bitcast.50, f32[2,128,128]{2,1,0:T(8,128)S(1)} %bitcast.52, bf16[256,128]{1,0:T(8,128)(2,1)S(1)} %copy-done.9, ...), custom_call_target="tpu_custom_call" | custom-call | tf_op jit(solution)/shard_map/transform/pallas_call | solution.py:91
  54.7 0.7 copy.39
  55.4 3.4 %all-to-all-start.3 = ((f32[8,2,16,128]{3,2,1,0:T(8,128)}), f32[8,2,16,128]{3,2,1,0:T(8,128)S(1)}, u32[]{:S(2)}, u32[]{:S(2)}) async-start(f32[8,2,16,128]{3,2,1,0:T(8,128)} %bitcast.49), calls=%async_computation.3 | async-start | bytes 262144 | tf_op jit(solution)/shard_map/all_to_all | solution.py:138
  58.7 0.1 maximum_bitcast_fusion.1
  58.8 1.2 %copy.23 = f32[4,8,2,2,16,128]{5,4,3,2,1,0:T(8,128)} copy(f32[4,8,2,2,16,128]{5,4,1,0,3,2:T(8,128)S(1)} %maximum_bitcast_fusion.1) | data formatting | bytes 2097152 | tf_op jit(solution)/shard_map/transpose | solution.py:144
  60.0 6.0 %all-to-all-done.3 = f32[8,2,16,128]{3,2,1,0:T(8,128)S(1)} async-done(((f32[8,2,16,128]{3,2,1,0:T(8,128)}), f32[8,2,16,128]{3,2,1,0:T(8,128)S(1)}, u32[]{:S(2)}, u32[]{:S(2)}) %all-to-all-start.3) | async-done | bytes 131104 | tf_op jit(solution)/shard_map/all_to_all | solution.py:138
  66.0 2.6 %all-to-all-start.2 = ((f32[32,2,2,16,128]{4,3,2,1,0:T(8,128)}), f32[32,2,2,16,128]{4,3,2,1,0:T(8,128)S(1)}, u32[]{:S(2)}, u32[]{:S(2)}) async-start(f32[32,2,2,16,128]{4,3,2,1,0:T(8,128)} %bitcast.10), calls=%async_computation.2 | async-start | bytes 2097152 | tf_op jit(solution)/shard_map/all_to_all | solution.py:145
  68.7 0.7 copy.38
  69.4 26.9 %all-to-all-done.2 = f32[32,2,2,16,128]{4,3,2,1,0:T(8,128)S(1)} async-done(((f32[32,2,2,16,128]{4,3,2,1,0:T(8,128)}), f32[32,2,2,16,128]{4,3,2,1,0:T(8,128)S(1)}, u32[]{:S(2)}, u32[]{:S(2)}) %all-to-all-start.2) | async-done | bytes 1048608 | tf_op jit(solution)/shard_map/all_to_all | solution.py:145
  96.3 1.2 %fusion.2 = (bf16[64,2048]{1,0:T(8,128)(2,1)}, bf16[64,2048]{1,0:T(8,128)(2,1)}, bf16[64,2048]{1,0:T(8,128)(2,1)}) fusion(bf16[64,2048]{1,0:T(8,128)(2,1)S(1)} %copy-done.10, f32[8,8,16,128]{3,2,1,0:T(8,128)S(1)} %bitcast.59, bf16[64,2048]{1,0:T(8,128)(2,1)S(1)} %copy-done.12, f32[8,8,16,128]{3,2,1,0:T(8,128)S(1)} %bitcast.60, bf16[64,2048]{1,0:T(8,128)(2,1)S(1)} %copy-done.11), kind=kLoop, calls=%fused_computation.10 | loop fusion | flops 1179648 | bytes 2621440 | tf_op jit(solution)/shard_map/convert_element_type | solution.py:150
  (29 shorter events, 0.6 us)
Async XLA Ops:
  0.6 1.0 %copy-start = (f32[64,2048]{1,0:T(8,128)S(1)}, f32[64,2048]{1,0:T(8,128)}, u32[]{:S(2)}) copy-start(f32[64,2048]{1,0:T(8,128)} %param.14) | copy-start | bytes 1572868
  1.7 8.0 %copy-start.11 = (bf16[64,2048]{1,0:T(8,128)(2,1)S(1)}, bf16[64,2048]{1,0:T(8,128)(2,1)}, u32[]{:S(2)}) copy-start(bf16[64,2048]{1,0:T(8,128)(2,1)} %param.13) | copy-start | bytes 786436
  1.7 8.0 %copy-start.13 = (bf16[64,2048]{1,0:T(8,128)(2,1)S(1)}, bf16[64,2048]{1,0:T(8,128)(2,1)}, u32[]{:S(2)}) copy-start(bf16[64,2048]{1,0:T(8,128)(2,1)} %param.10) | copy-start | bytes 786436
  2.4 14.6 %all-to-all-start.1 = ((f32[8,2,16,128]{3,2,1,0:T(8,128)}), f32[8,2,16,128]{3,2,1,0:T(8,128)S(1)}, u32[]{:S(2)}, u32[]{:S(2)}) async-start(f32[8,2,16,128]{3,2,1,0:T(8,128)} %bitcast.24), calls=%async_computation.1 | async-start | bytes 262144 | tf_op jit(solution)/shard_map/all_to_all | solution.py:133
  9.7 1.0 copy-start.10
  9.7 1.0 %copy-start.12 = (bf16[64,2048]{1,0:T(8,128)(2,1)S(1)}, bf16[64,2048]{1,0:T(8,128)(2,1)}, u32[]{:S(2)}) copy-start(bf16[64,2048]{1,0:T(8,128)(2,1)} %param.12) | copy-start | bytes 786436
  17.0 30.2 %all-to-all-start = ((f32[32,2,2,16,128]{4,3,2,1,0:T(8,128)}), f32[32,2,2,16,128]{4,3,2,1,0:T(8,128)S(1)}, u32[]{:S(2)}, u32[]{:S(2)}) async-start(f32[32,2,2,16,128]{4,3,2,1,0:T(8,128)} %maximum_bitcast_fusion), calls=%async_computation | async-start | bytes 2097152 | tf_op jit(solution)/shard_map/all_to_all | solution.py:124
  47.4 0.9 copy-start.1
  47.4 1.0 copy-start.2
  47.4 1.0 %copy-start.3 = (bf16[256,256]{1,0:T(8,128)(2,1)S(1)}, bf16[256,256]{1,0:T(8,128)(2,1)}, u32[]{:S(2)}) copy-start(bf16[256,256]{1,0:T(8,128)(2,1)} %constant.32.second_lo) | copy-start | bytes 393220
  47.4 1.1 %copy-start.4 = (bf16[256,256]{1,0:T(8,128)(2,1)S(1)}, bf16[256,256]{1,0:T(8,128)(2,1)}, u32[]{:S(2)}) copy-start(bf16[256,256]{1,0:T(8,128)(2,1)} %constant.29.second_hi) | copy-start | bytes 393220
  47.4 1.1 %copy-start.5 = (f32[2,128,128]{2,1,0:T(8,128)S(1)}, f32[2,128,128]{2,1,0:T(8,128)}, u32[]{:S(2)}) copy-start(f32[2,128,128]{2,1,0:T(8,128)} %constant.24.clone.twist_ref) | copy-start | bytes 393220
  47.4 1.1 %copy-start.6 = (bf16[128,256]{1,0:T(8,128)(2,1)S(1)}, bf16[128,256]{1,0:T(8,128)(2,1)}, u32[]{:S(2)}) copy-start(bf16[128,256]{1,0:T(8,128)(2,1)} %constant.40.last_lo) | copy-start | bytes 196612
  47.5 1.1 %copy-start.7 = (bf16[128,256]{1,0:T(8,128)(2,1)S(1)}, bf16[128,256]{1,0:T(8,128)(2,1)}, u32[]{:S(2)}) copy-start(bf16[128,256]{1,0:T(8,128)(2,1)} %constant.37.last_hi) | copy-start | bytes 196612
  47.5 1.1 %copy-start.8 = (bf16[256,128]{1,0:T(8,128)(2,1)S(1)}, bf16[256,128]{1,0:T(8,128)(2,1)}, u32[]{:S(2)}) copy-start(bf16[256,128]{1,0:T(8,128)(2,1)} %constant.28.first_lo) | copy-start | bytes 196612
  47.5 1.1 %copy-start.9 = (bf16[256,128]{1,0:T(8,128)(2,1)S(1)}, bf16[256,128]{1,0:T(8,128)(2,1)}, u32[]{:S(2)}) copy-start(bf16[256,128]{1,0:T(8,128)(2,1)} %constant.25.first_hi) | copy-start | bytes 196612
  55.4 10.7 %all-to-all-start.3 = ((f32[8,2,16,128]{3,2,1,0:T(8,128)}), f32[8,2,16,128]{3,2,1,0:T(8,128)S(1)}, u32[]{:S(2)}, u32[]{:S(2)}) async-start(f32[8,2,16,128]{3,2,1,0:T(8,128)} %bitcast.49), calls=%async_computation.3 | async-start | bytes 262144 | tf_op jit(solution)/shard_map/all_to_all | solution.py:138
  66.0 30.2 %all-to-all-start.2 = ((f32[32,2,2,16,128]{4,3,2,1,0:T(8,128)}), f32[32,2,2,16,128]{4,3,2,1,0:T(8,128)S(1)}, u32[]{:S(2)}, u32[]{:S(2)}) async-start(f32[32,2,2,16,128]{4,3,2,1,0:T(8,128)} %bitcast.10), calls=%async_computation.2 | async-start | bytes 2097152 | tf_op jit(solution)/shard_map/all_to_all | solution.py:145

commit v2 on v1

v2 whole, which is shorter than its diff:
```python
import functools
import math

import jax
import jax.numpy as jnp
import numpy as np
from jax import lax
from jax.experimental import pallas as pl
from jax.experimental.pallas import tpu as pltpu
from jax.sharding import PartitionSpec as P


def split_bf16(value):
    high = value.astype(jnp.bfloat16)
    return high, (value - high.astype(jnp.float32)).astype(jnp.bfloat16)


def tables(rows, cols):
    total = rows * cols
    row = np.arange(rows)
    col = np.arange(cols)
    angle = 2.0 * np.pi * ((4 * row[:, None] + 1) * row[None, :] % (4 * rows)) / (4 * rows)
    first = np.concatenate([np.cos(angle), -np.sin(angle)], axis=0)
    angle = 2.0 * np.pi * (col[:, None] * col[None, :] % cols) / cols
    cos, sin = np.cos(angle), np.sin(angle)
    second = np.block([[cos, -sin], [sin, cos]])
    angle = 2.0 * np.pi * ((4 * row[:, None] + 1) * col[None, :]) / (4 * total)
    twist = np.stack([np.cos(angle), -np.sin(angle)]).astype(np.float32)
    out = []
    for table in (first, second, second.T, first.T / total):
        out += list(split_bf16(jnp.asarray(table.astype(np.float32))))
    return out + [jnp.asarray(twist)]


def product(left, right):
    dot = functools.partial(jnp.dot, preferred_element_type=jnp.float32)
    return dot(left[0], right[0]) + dot(left[0], right[1]) + dot(left[1], right[0])


def transform_channels(tables_in, mixed, gated, taps, scale):
    first, second, back, last, twist_re, twist_im = tables_in
    rows, cols = twist_re.shape

    def forward(block):
        part = product(first, split_bf16(block))
        re, im = part[:rows], part[rows:]
        turned = jnp.concatenate(
            [re * twist_re - im * twist_im, re * twist_im + im * twist_re], axis=1
        )
        spec = product(split_bf16(turned), second)
        return spec[:, :cols], spec[:, cols:]

    def inverse(re, im):
        part = product(split_bf16(jnp.concatenate([re, im], axis=1)), back)
        re, im = part[:, :cols], part[:, cols:]
        turned = jnp.concatenate(
            [re * twist_re + im * twist_im, im * twist_re - re * twist_im], axis=0
        )
        return product(last, split_bf16(turned))

    h_re, h_im = forward(taps())
    k_re = k_im = 0.0
    pairs = []
    for mixed_one, gated_one in zip(mixed, gated):
        m_re, m_im = forward(mixed_one())
        g_re, g_im = forward(gated_one())
        response = inverse(h_re * m_re - h_im * m_im, h_re * m_im + h_im * m_re)
        grad = inverse(h_re * g_re + h_im * g_im, h_re * g_im - h_im * g_re)
        k_re += m_re * g_re + m_im * g_im
        k_im += m_re * g_im - m_im * g_re
        pairs.append((response, grad))
    return pairs, inverse(k_re, k_im) * scale


def exchange_kernel(
    repeat, seq_count, held, scale,
    send_ref, taps_ref,
    first_hi, first_lo, second_hi, second_lo, back_hi, back_lo, last_hi, last_lo, twist_ref,
    result_ref, kernel_ref,
    seqs, taps_all, outs, kernels,
    in_sem, taps_sem, out_sem, kernel_sem, in_sent, taps_sent, out_sent, kernel_sent,
):
    parts = repeat * seq_count
    rows_dev = taps_ref.shape[-2]
    seq_me = lax.axis_index("seq")
    chan_me = lax.axis_index("chan")
    place_me = seq_me + (chan_me * seq_count if repeat > 1 else 0)
    source_me = chan_me if repeat > 1 else 0

    def device(part):
        chan = part // seq_count if repeat > 1 else chan_me
        return {"seq": part % seq_count, "chan": chan}

    def chan_of(part):
        return part // seq_count if repeat > 1 else 0

    def span(seq):
        return pl.ds(pl.multiple_of(seq * rows_dev, rows_dev), rows_dev)

    def peer(step):
        return lax.rem(place_me + step, parts)

    def seq_peer(step):
        return lax.rem(seq_me + step, seq_count)

    barrier = pltpu.get_barrier_semaphore()

    @pl.loop(1, parts)
    def _(step):
        pl.semaphore_signal(
            barrier, inc=1, device_id=device(peer(step)), device_id_type=pl.DeviceIdType.MESH
        )

    pl.semaphore_wait(barrier, parts - 1)

    def send_in(index):
        pltpu.make_async_copy(
            taps_ref.at[seq_me, index], taps_all.at[index, span(seq_me)], taps_sem.at[index]
        ).start()

        @pl.loop(1, seq_count)
        def _(step):
            to = seq_peer(step)
            pltpu.make_async_remote_copy(
                src_ref=taps_ref.at[to, index],
                dst_ref=taps_all.at[index, span(seq_me)],
                send_sem=taps_sent.at[index],
                recv_sem=taps_sem.at[index],
                device_id={"seq": to, "chan": chan_me},
                device_id_type=pl.DeviceIdType.MESH,
            ).start()

        pltpu.make_async_copy(
            send_ref.at[place_me, index],
            seqs.at[index, :, source_me, span(seq_me)],
            in_sem.at[index],
        ).start()

        @pl.loop(1, parts)
        def _(step):
            to = peer(step)
            pltpu.make_async_remote_copy(
                src_ref=send_ref.at[to, index],
                dst_ref=seqs.at[index, :, source_me, span(seq_me)],
                send_sem=in_sent.at[index],
                recv_sem=in_sem.at[index],
                device_id=device(to),
                device_id_type=pl.DeviceIdType.MESH,
            ).start()

    def send_out(index):
        mine = place_me * held + index
        pltpu.make_async_copy(
            kernels.at[index, span(seq_me)],
            kernel_ref.at[seq_me * held + index],
            kernel_sem,
        ).start()

        @pl.loop(1, seq_count)
        def _(step):
            to = seq_peer(step)
            pltpu.make_async_remote_copy(
                src_ref=kernels.at[index, span(to)],
                dst_ref=kernel_ref.at[seq_me * held + index],
                send_sem=kernel_sent.at[index],
                recv_sem=kernel_sem,
                device_id={"seq": to, "chan": chan_me},
                device_id_type=pl.DeviceIdType.MESH,
            ).start()

        pltpu.make_async_copy(
            outs.at[index, :, source_me, span(seq_me)], result_ref.at[:, mine], out_sem
        ).start()

        @pl.loop(1, parts)
        def _(step):
            to = peer(step)
            pltpu.make_async_remote_copy(
                src_ref=outs.at[index, :, chan_of(to), span(to % seq_count)],
                dst_ref=result_ref.at[:, mine],
                send_sem=out_sent.at[index],
                recv_sem=out_sem,
                device_id=device(to),
                device_id_type=pl.DeviceIdType.MESH,
            ).start()

    def finish(ref, sem):
        pltpu.make_async_copy(ref, ref, sem).wait()

    for index in range(held):
        send_in(index)

    tables_in = (
        (first_hi[...], first_lo[...]),
        (second_hi[...], second_lo[...]),
        (back_hi[...], back_lo[...]),
        (last_hi[...], last_lo[...]),
        twist_ref[0],
        twist_ref[1],
    )

    for index in range(held):
        finish(taps_all.at[index], taps_sem.at[index])
        finish(seqs.at[index], in_sem.at[index])
        mixed = [functools.partial(lambda c: seqs[index, 0, c], c) for c in range(repeat)]
        gated = [functools.partial(lambda c: seqs[index, 1, c], c) for c in range(repeat)]
        pairs, kernel = transform_channels(
            tables_in, mixed, gated, lambda: taps_all[index], scale
        )
        for chan, (response, grad) in enumerate(pairs):
            outs[index, 0, chan] = response
            outs[index, 1, chan] = grad
        kernels[index] = kernel
        send_out(index)

    for index in range(held):
        finish(send_ref.at[pl.ds(0, parts - 1), index], in_sent.at[index])
        finish(taps_ref.at[pl.ds(0, seq_count - 1), index], taps_sent.at[index])
        finish(send_ref.at[pl.ds(0, parts - 1), index], out_sent.at[index])
        finish(taps_ref.at[pl.ds(0, seq_count - 1), index], kernel_sent.at[index])
    finish(kernel_ref, kernel_sem)
    finish(result_ref, out_sem)


def exchange(send, taps, repeat, rows, cols):
    parts, held, _, rows_dev, _ = send.shape
    seq_count = parts // repeat
    constants = tables(rows, cols)
    vmem = pl.BlockSpec(memory_space=pltpu.VMEM)
    hbm = pl.BlockSpec(memory_space=pl.ANY)
    f32 = jnp.float32
    dma = pltpu.SemaphoreType.DMA
    moved = 2 * 4 * (send.size + taps.size)
    return pl.pallas_call(
        functools.partial(
            exchange_kernel, repeat, seq_count, held, 1.0 / math.sqrt(rows * cols)
        ),
        in_specs=[vmem] * (2 + len(constants)),
        out_specs=[hbm, hbm],
        out_shape=[
            jax.ShapeDtypeStruct((2, parts * held, rows_dev, cols), f32),
            jax.ShapeDtypeStruct((seq_count * held, rows_dev, cols), f32),
        ],
        scratch_shapes=[
            pltpu.VMEM((held, 2, repeat, rows, cols), f32),
            pltpu.VMEM((held, rows, cols), f32),
            pltpu.VMEM((held, 2, repeat, rows, cols), f32),
            pltpu.VMEM((held, rows, cols), f32),
            dma((held,)), dma((held,)), dma(()), dma(()),
            dma((held,)), dma((held,)), dma((held,)), dma((held,)),
        ],
        compiler_params=pltpu.CompilerParams(
            collective_id=0, has_side_effects=True, vmem_limit_bytes=48 * 1024 * 1024
        ),
        cost_estimate=pl.CostEstimate(
            flops=12 * send.size * (rows + cols) * 4, bytes_accessed=moved, transcendentals=0
        ),
        name="exchange",
    )(send, taps, *constants)


def per_device(output_gate, input_gate, signal, cotangent, long_filter):
    seq_count = lax.axis_size("seq")
    chan_count = lax.axis_size("chan")
    channels, tok_local = signal.shape
    filters = long_filter.shape[0]
    tokens = tok_local * seq_count
    cols = 2 ** (int(math.log2(tokens)) // 2)
    rows = tokens // cols
    rows_dev = rows // seq_count
    spread = channels == filters and filters % (seq_count * chan_count) == 0
    repeat = chan_count if spread else 1
    parts = seq_count * repeat
    held = filters // parts

    mixed = input_gate.astype(jnp.float32) * signal.astype(jnp.float32)
    gated = cotangent.astype(jnp.float32) * output_gate.astype(jnp.float32)
    send = jnp.stack([mixed, gated], axis=0).reshape(2, parts, held, rows_dev, cols)
    send = send.transpose(1, 2, 0, 3, 4)
    if spread:
        block = held * seq_count
        long_filter = lax.dynamic_slice_in_dim(
            long_filter, lax.axis_index("chan") * block, block, axis=0
        )
    taps = long_filter.reshape(seq_count, held, rows_dev, cols)

    results, kernel = exchange(send, taps, repeat, rows, cols)

    kernel = kernel.reshape(held * seq_count, tok_local)
    if not spread:
        kernel = lax.psum_scatter(kernel, "chan", scatter_dimension=0, tiled=True)
    response, grad_mixed = results.reshape(2, channels, tok_local)
    grad_output_gate = (cotangent.astype(jnp.float32) * response).astype(jnp.bfloat16)
    grad_input_gate = (grad_mixed * signal.astype(jnp.float32)).astype(jnp.bfloat16)
    grad_signal = (grad_mixed * input_gate.astype(jnp.float32)).astype(jnp.bfloat16)
    return (grad_output_gate, grad_input_gate, grad_signal, kernel)


def solution(mesh):
    placed = (
        P("chan", "seq"),
        P("chan", "seq"),
        P("chan", "seq"),
        P("chan", "seq"),
        P(None, "seq"),
    )
    return jax.shard_map(
        per_device,
        mesh=mesh,
        in_specs=placed,
        out_specs=(P("chan", "seq"), P("chan", "seq"), P("chan", "seq"), P("chan", "seq")),
        check_vma=False,
    )
```

time: 98.1 us -> 66 us (0.67)
  waiting for transfers between devices: 65.4 us -> 0 us
  Pallas kernels: 6.1 us -> 58.6 us
  starting transfers between devices: 15.9 us -> 0 us
  local copies, waits for them, and re-layouts: 6.73 us -> 4.97 us
  other arithmetic: 2.5 us -> 1.39 us
    all_to_all x4 -> x0, waiting for transfers between devices: 65.4 us -> none  [the longest x1 27.6 us: per_device(): pieces = lax.all_to_all(stacked.transpose(1, 0, 2, 3, 4), axes, 0, 0)]
    pallas_call x1, Pallas kernels: 6.1 us -> 58.6 us  [exchange(): pl.pallas_call(functools.partial(exchange_kernel, repeat, seq_count, held...]
    all_to_all x4 -> x0, starting transfers between devices: 15.9 us -> none  [the longest x1 7.28 us: per_device(): lax.all_to_all(taps, 'seq', 0, 0).transpose(1, 0, 2, 3)]
    transpose x2 -> x0, local copies, waits for them, and re-layouts: 1.17 us -> none  [the longest x1 1.16 us: per_device(): results.transpose(2, 3, 0, 1, 4, 5).reshape(parts, 2, held, rows_dev, cols)]
    transpose x2 -> x1, other arithmetic: 1.19 us -> 0.09 us  [per_device(): send = send.transpose(1, 2, 0, 3, 4)]
  transfers between devices with their start and end apart: 4 -> 0, of which waited for: 4 -> 0; matrix products, arithmetic and copies ran while one was open for 3% -> 0% of each run, Pallas kernels for 0% -> 0%
where the time goes in v2:
time: 66 us; the launch traced here: 65.8 us
  Pallas kernels  58.6 us (89%)
  local copies, waits for them, and re-layouts  4.97 us (8%)
  other arithmetic  1.39 us (2%)
  between operations  0.79 us (1%)
    pallas_call x1, Pallas kernels, exchange(): pl.pallas_call(functools.partial(exchange_kernel, repeat, seq_count, held...  58.6 us
    unnamed x33, local copies, waits for them, and re-layouts  4.9 us

profile of v2, /device:TPU:0, one launch (start us, length us, event | category | flops | bytes accessed | tf_op | source)
XLA Modules:
  0.0 65.8 jit_solution(10594576445961098084)
XLA Ops:
  0.6 0.0 copy-start
  0.7 1.0 %copy-done = f32[64,2048]{1,0:T(8,128)S(1)} copy-done((f32[64,2048]{1,0:T(8,128)S(1)}, f32[64,2048]{1,0:T(8,128)}, u32[]{:S(2)}) %copy-start) | copy-done | bytes 524312
  1.7 0.9 %copy-done.11 = bf16[64,2048]{1,0:T(8,128)(2,1)S(1)} copy-done((bf16[64,2048]{1,0:T(8,128)(2,1)S(1)}, bf16[64,2048]{1,0:T(8,128)(2,1)}, u32[]{:S(2)}) %copy-start.11) | copy-done | bytes 262168
  2.6 0.1 copy-done.13
  2.7 0.1 fusion
  2.8 0.1 copy.15
  2.9 0.8 %copy-done.10 = bf16[64,2048]{1,0:T(8,128)(2,1)S(1)} copy-done((bf16[64,2048]{1,0:T(8,128)(2,1)S(1)}, bf16[64,2048]{1,0:T(8,128)(2,1)}, u32[]{:S(2)}) %copy-start.10) | copy-done | bytes 262168
  3.7 0.1 copy-done.12
  3.8 0.1 fusion.3
  3.9 0.1 copy.14
  4.0 0.0 copy-start.1
  4.0 0.0 copy-start.2
  4.1 0.1 maximum_bitcast_fusion.send_ref
  4.2 0.7 %copy-done.1 = bf16[256,256]{1,0:T(8,128)(2,1)S(1)} copy-done((bf16[256,256]{1,0:T(8,128)(2,1)S(1)}, bf16[256,256]{1,0:T(8,128)(2,1)}, u32[]{:S(2)}) %copy-start.1) | copy-done | bytes 131096
  4.9 0.1 copy-done.2
  4.9 0.1 copy-done.3
  5.0 0.1 copy-done.4
  5.1 0.1 copy-done.5
  5.1 0.0 copy-done.8
  5.2 0.0 copy-done.9
  5.2 58.6 %exchange.1 = (f32[2,64,16,128]{3,2,1,0:T(8,128)S(1)}, f32[16,16,128]{2,1,0:T(8,128)S(1)}) custom-call(f32[32,2,2,16,128]{4,3,2,1,0:T(8,128)S(1)} %maximum_bitcast_fusion.send_ref, f32[8,2,16,128]{3,2,1,0:T(8,128)S(1)} %bitcast.29, bf16[256,128]{1,0:T(8,128)(2,1)S(1)} %copy-done.9, bf16[256,128]{1,0:T(8,128)(2,1)S(1)} %copy-done.8, ...), custom_call_target="tpu_custom_call" | custom-call | flops 3221225472 | bytes 2359296 | tf_op jit(solution)/shard_map/exchange/pallas_call | solution.py:234
  63.8 0.7 %copy.24 = f32[2,8,16,128]{3,1,2,0:T(8,128)} copy(f32[2,8,16,128]{3,2,1,0:T(8,128)S(1)} %bitcast.30) | data formatting | bytes 262144
  64.5 0.1 fusion.5
  64.6 1.2 %fusion.2 = (bf16[64,2048]{1,0:T(8,128)(2,1)}, bf16[64,2048]{1,0:T(8,128)(2,1)}, bf16[64,2048]{1,0:T(8,128)(2,1)}) fusion(bf16[64,2048]{1,0:T(8,128)(2,1)S(1)} %copy-done.10, f32[8,8,16,128]{3,2,1,0:T(8,128)S(1)} %bitcast.31, bf16[64,2048]{1,0:T(8,128)(2,1)S(1)} %copy-done.12, f32[8,8,16,128]{3,2,1,0:T(8,128)S(1)} %bitcast.32, bf16[64,2048]{1,0:T(8,128)(2,1)S(1)} %copy-done.11), kind=kLoop, calls=%fused_computation.8 | loop fusion | flops 1179648 | bytes 2621440 | tf_op jit(solution)/shard_map/convert_element_type | solution.py:295
  (15 shorter events, 0.1 us)
Async XLA Ops:
  0.6 1.0 %copy-start = (f32[64,2048]{1,0:T(8,128)S(1)}, f32[64,2048]{1,0:T(8,128)}, u32[]{:S(2)}) copy-start(f32[64,2048]{1,0:T(8,128)} %param.14) | copy-start | bytes 1572868
  1.7 0.9 %copy-start.11 = (bf16[64,2048]{1,0:T(8,128)(2,1)S(1)}, bf16[64,2048]{1,0:T(8,128)(2,1)}, u32[]{:S(2)}) copy-start(bf16[64,2048]{1,0:T(8,128)(2,1)} %param.13) | copy-start | bytes 786436
  1.7 1.0 %copy-start.13 = (bf16[64,2048]{1,0:T(8,128)(2,1)S(1)}, bf16[64,2048]{1,0:T(8,128)(2,1)}, u32[]{:S(2)}) copy-start(bf16[64,2048]{1,0:T(8,128)(2,1)} %param.10) | copy-start | bytes 786436
  2.8 1.0 %copy-start.10 = (bf16[64,2048]{1,0:T(8,128)(2,1)S(1)}, bf16[64,2048]{1,0:T(8,128)(2,1)}, u32[]{:S(2)}) copy-start(bf16[64,2048]{1,0:T(8,128)(2,1)} %param.11) | copy-start | bytes 786436
  2.8 1.0 %copy-start.12 = (bf16[64,2048]{1,0:T(8,128)(2,1)S(1)}, bf16[64,2048]{1,0:T(8,128)(2,1)}, u32[]{:S(2)}) copy-start(bf16[64,2048]{1,0:T(8,128)(2,1)} %param.12) | copy-start | bytes 786436
  4.0 0.9 %copy-start.1 = (bf16[256,256]{1,0:T(8,128)(2,1)S(1)}, bf16[256,256]{1,0:T(8,128)(2,1)}, u32[]{:S(2)}) copy-start(bf16[256,256]{1,0:T(8,128)(2,1)} %constant.36.back_lo) | copy-start | bytes 393220
  4.0 1.0 %copy-start.2 = (bf16[256,256]{1,0:T(8,128)(2,1)S(1)}, bf16[256,256]{1,0:T(8,128)(2,1)}, u32[]{:S(2)}) copy-start(bf16[256,256]{1,0:T(8,128)(2,1)} %constant.33.back_hi) | copy-start | bytes 393220
  4.0 1.0 %copy-start.3 = (bf16[256,256]{1,0:T(8,128)(2,1)S(1)}, bf16[256,256]{1,0:T(8,128)(2,1)}, u32[]{:S(2)}) copy-start(bf16[256,256]{1,0:T(8,128)(2,1)} %constant.32.second_lo) | copy-start | bytes 393220
  4.0 1.1 %copy-start.4 = (bf16[256,256]{1,0:T(8,128)(2,1)S(1)}, bf16[256,256]{1,0:T(8,128)(2,1)}, u32[]{:S(2)}) copy-start(bf16[256,256]{1,0:T(8,128)(2,1)} %constant.29.second_hi) | copy-start | bytes 393220
  4.0 1.1 %copy-start.5 = (f32[2,128,128]{2,1,0:T(8,128)S(1)}, f32[2,128,128]{2,1,0:T(8,128)}, u32[]{:S(2)}) copy-start(f32[2,128,128]{2,1,0:T(8,128)} %constant.24.clone.twist_ref) | copy-start | bytes 393220
  4.0 1.1 %copy-start.6 = (bf16[128,256]{1,0:T(8,128)(2,1)S(1)}, bf16[128,256]{1,0:T(8,128)(2,1)}, u32[]{:S(2)}) copy-start(bf16[128,256]{1,0:T(8,128)(2,1)} %constant.40.last_lo) | copy-start | bytes 196612
  4.0 1.1 %copy-start.7 = (bf16[128,256]{1,0:T(8,128)(2,1)S(1)}, bf16[128,256]{1,0:T(8,128)(2,1)}, u32[]{:S(2)}) copy-start(bf16[128,256]{1,0:T(8,128)(2,1)} %constant.37.last_hi) | copy-start | bytes 196612
  4.1 1.1 %copy-start.8 = (bf16[256,128]{1,0:T(8,128)(2,1)S(1)}, bf16[256,128]{1,0:T(8,128)(2,1)}, u32[]{:S(2)}) copy-start(bf16[256,128]{1,0:T(8,128)(2,1)} %constant.28.first_lo) | copy-start | bytes 196612
  4.1 1.1 %copy-start.9 = (bf16[256,128]{1,0:T(8,128)(2,1)S(1)}, bf16[256,128]{1,0:T(8,128)(2,1)}, u32[]{:S(2)}) copy-start(bf16[256,128]{1,0:T(8,128)(2,1)} %constant.25.first_hi) | copy-start | bytes 196612

commit v3 on v2

--- a/solution.py
+++ b/solution.py
@@ -73,15 +73,21 @@
 
 
 def exchange_kernel(
-    repeat, seq_count, held, scale,
-    send_ref, taps_ref,
-    first_hi, first_lo, second_hi, second_lo, back_hi, back_lo, last_hi, last_lo, twist_ref,
-    result_ref, kernel_ref,
-    seqs, taps_all, outs, kernels,
-    in_sem, taps_sem, out_sem, kernel_sem, in_sent, taps_sent, out_sent, kernel_sent,
+    repeat, seq_count, held, rows_dev, scale,
+    output_gate_ref, input_gate_ref, signal_ref, cotangent_ref, filter_ref, *refs,
 ):
+    constants = refs[:9]
+    result_ref, kernel_ref = refs[9:11]
+    tables_ref = refs[11:20]
+    (
+        output_gate, input_gate, signal, cotangent, filter_rows, send_ref, taps_ref,
+        seqs, taps_all, outs, kernels,
+        load_sem, table_sem, in_sem, taps_sem, out_sem, kernel_sem,
+        in_sent, taps_sent, out_sent, kernel_sent,
+    ) = refs[20:]
     parts = repeat * seq_count
-    rows_dev = taps_ref.shape[-2]
+    wide = 2 * rows_dev
+    channels = signal.shape[0]
     seq_me = lax.axis_index("seq")
     chan_me = lax.axis_index("chan")
     place_me = seq_me + (chan_me * seq_count if repeat > 1 else 0)
@@ -97,11 +103,38 @@
     def span(seq):
         return pl.ds(pl.multiple_of(seq * rows_dev, rows_dev), rows_dev)
 
+    def wide_span(block):
+        return pl.ds(pl.multiple_of(block * wide, wide), wide)
+
     def peer(step):
-        return lax.rem(place_me + step, parts)
+        turn = lax.rem(seq_me * repeat + source_me + step, parts)
+        return (turn % repeat) * seq_count + turn // repeat
 
     def seq_peer(step):
         return lax.rem(seq_me + step, seq_count)
+
+    block = held * seq_count
+    first_filter = pl.multiple_of(source_me * block, block)
+    loads = [
+        pltpu.make_async_copy(
+            filter_ref.at[pl.ds(first_filter, block)], filter_rows, load_sem.at[4]
+        )
+    ]
+    for place, (source, target) in enumerate(
+        (
+            (output_gate_ref, output_gate),
+            (input_gate_ref, input_gate),
+            (signal_ref, signal),
+            (cotangent_ref, cotangent),
+        )
+    ):
+        loads.append(pltpu.make_async_copy(source, target, load_sem.at[place]))
+    table_loads = [
+        pltpu.make_async_copy(source, target, table_sem.at[place])
+        for place, (source, target) in enumerate(zip(constants, tables_ref))
+    ]
+    for load in loads + table_loads:
+        load.start()
 
     barrier = pltpu.get_barrier_semaphore()
 
@@ -111,18 +144,43 @@
             barrier, inc=1, device_id=device(peer(step)), device_id_type=pl.DeviceIdType.MESH
         )
 
+    for load in loads:
+        load.wait()
+
+    @pl.loop(0, block // 8)
+    def _(group):
+        for row in range(rows_dev):
+            taps_ref[pl.ds(group * (8 * rows_dev) + row, 8, stride=rows_dev)] = filter_rows[
+                pl.ds(pl.multiple_of(group * 8, 8), 8), pl.ds(row * 128, 128)
+            ]
+
+    @pl.loop(0, channels // 16)
+    def _(group):
+        lines = pl.ds(pl.multiple_of(group * 16, 16), 16)
+        for row in range(rows_dev):
+            lanes = pl.ds(row * 128, 128)
+            mixed = input_gate[lines, lanes].astype(jnp.float32) * signal[lines, lanes].astype(
+                jnp.float32
+            )
+            gated = cotangent[lines, lanes].astype(jnp.float32) * output_gate[
+                lines, lanes
+            ].astype(jnp.float32)
+            start = group * (16 * wide) + row
+            send_ref[pl.ds(start, 16, stride=wide)] = mixed
+            send_ref[pl.ds(start + rows_dev, 16, stride=wide)] = gated
+
     pl.semaphore_wait(barrier, parts - 1)
 
     def send_in(index):
         pltpu.make_async_copy(
-            taps_ref.at[seq_me, index], taps_all.at[index, span(seq_me)], taps_sem.at[index]
+            taps_ref.at[span(seq_me * held + index)], taps_all.at[index, span(seq_me)], taps_sem.at[index]
         ).start()
 
         @pl.loop(1, seq_count)
         def _(step):
             to = seq_peer(step)
             pltpu.make_async_remote_copy(
-                src_ref=taps_ref.at[to, index],
+                src_ref=taps_ref.at[span(to * held + index)],
                 dst_ref=taps_all.at[index, span(seq_me)],
                 send_sem=taps_sent.at[index],
                 recv_sem=taps_sem.at[index],
@@ -131,8 +189,8 @@
             ).start()
 
         pltpu.make_async_copy(
-            send_ref.at[place_me, index],
-            seqs.at[index, :, source_me, span(seq_me)],
+            send_ref.at[wide_span(place_me * held + index)],
+            seqs.at[index, source_me, wide_span(seq_me)],
             in_sem.at[index],
         ).start()
 
@@ -140,8 +198,8 @@
         def _(step):
             to = peer(step)
             pltpu.make_async_remote_copy(
-                src_ref=send_ref.at[to, index],
-                dst_ref=seqs.at[index, :, source_me, span(seq_me)],
+                src_ref=send_ref.at[wide_span(to * held + index)],
+                dst_ref=seqs.at[index, source_me, wide_span(seq_me)],
                 send_sem=in_sent.at[index],
                 recv_sem=in_sem.at[index],
                 device_id=device(to),
@@ -190,20 +248,20 @@
     for index in range(held):
         send_in(index)
 
-    tables_in = (
-        (first_hi[...], first_lo[...]),
-        (second_hi[...], second_lo[...]),
-        (back_hi[...], back_lo[...]),
-        (last_hi[...], last_lo[...]),
-        twist_ref[0],
-        twist_ref[1],
-    )
+    for load in table_loads:
+        load.wait()
+    whole = [table[...] for table in tables_ref[:8]]
+    tables_in = tuple(zip(whole[::2], whole[1::2])) + (tables_ref[8][0], tables_ref[8][1])
+
+    def sequence(index, which, chan):
+        lines = seqs[index, chan].reshape(seq_count, 2, rows_dev, 128)
+        return lines[:, which].reshape(seq_count * rows_dev, 128)
 
     for index in range(held):
         finish(taps_all.at[index], taps_sem.at[index])
         finish(seqs.at[index], in_sem.at[index])
-        mixed = [functools.partial(lambda c: seqs[index, 0, c], c) for c in range(repeat)]
-        gated = [functools.partial(lambda c: seqs[index, 1, c], c) for c in range(repeat)]
+        mixed = [functools.partial(sequence, index, 0, c) for c in range(repeat)]
+        gated = [functools.partial(sequence, index, 1, c) for c in range(repeat)]
         pairs, kernel = transform_channels(
             tables_in, mixed, gated, lambda: taps_all[index], scale
         )
@@ -214,49 +272,56 @@
         send_out(index)
 
     for index in range(held):
-        finish(send_ref.at[pl.ds(0, parts - 1), index], in_sent.at[index])
-        finish(taps_ref.at[pl.ds(0, seq_count - 1), index], taps_sent.at[index])
-        finish(send_ref.at[pl.ds(0, parts - 1), index], out_sent.at[index])
-        finish(taps_ref.at[pl.ds(0, seq_count - 1), index], kernel_sent.at[index])
+        finish(send_ref.at[pl.ds(0, (parts - 1) * wide)], in_sent.at[index])
+        finish(taps_ref.at[pl.ds(0, (seq_count - 1) * rows_dev)], taps_sent.at[index])
+        finish(send_ref.at[pl.ds(0, (parts - 1) * wide)], out_sent.at[index])
+        finish(taps_ref.at[pl.ds(0, (seq_count - 1) * rows_dev)], kernel_sent.at[index])
     finish(kernel_ref, kernel_sem)
     finish(result_ref, out_sem)
 
 
-def exchange(send, taps, repeat, rows, cols):
-    parts, held, _, rows_dev, _ = send.shape
-    seq_count = parts // repeat
-    constants = tables(rows, cols)
-    vmem = pl.BlockSpec(memory_space=pltpu.VMEM)
+def exchange(inputs, repeat, seq_count, held):
+    channels, tok_local = inputs[2].shape
+    rows_dev = tok_local // 128
+    rows = rows_dev * seq_count
+    parts = repeat * seq_count
+    constants = tables(rows, 128)
     hbm = pl.BlockSpec(memory_space=pl.ANY)
     f32 = jnp.float32
     dma = pltpu.SemaphoreType.DMA
-    moved = 2 * 4 * (send.size + taps.size)
+    size = 2 * channels * tok_local
     return pl.pallas_call(
         functools.partial(
-            exchange_kernel, repeat, seq_count, held, 1.0 / math.sqrt(rows * cols)
+            exchange_kernel, repeat, seq_count, held, rows_dev, 1.0 / math.sqrt(rows * 128)
         ),
-        in_specs=[vmem] * (2 + len(constants)),
+        in_specs=[hbm] * (5 + len(constants)),
         out_specs=[hbm, hbm],
         out_shape=[
-            jax.ShapeDtypeStruct((2, parts * held, rows_dev, cols), f32),
-            jax.ShapeDtypeStruct((seq_count * held, rows_dev, cols), f32),
+            jax.ShapeDtypeStruct((2, channels, rows_dev, 128), f32),
+            jax.ShapeDtypeStruct((seq_count * held, rows_dev, 128), f32),
         ],
-        scratch_shapes=[
-            pltpu.VMEM((held, 2, repeat, rows, cols), f32),
-            pltpu.VMEM((held, rows, cols), f32),
-            pltpu.VMEM((held, 2, repeat, rows, cols), f32),
-            pltpu.VMEM((held, rows, cols), f32),
+        scratch_shapes=[pltpu.VMEM(table.shape, table.dtype) for table in constants]
+        + [pltpu.VMEM((channels, tok_local), jnp.bfloat16)] * 4
+        + [
+            pltpu.VMEM((held * seq_count, tok_local), f32),
+            pltpu.VMEM((channels * 2 * rows_dev, 128), f32),
+            pltpu.VMEM((held * seq_count * rows_dev, 128), f32),
+            pltpu.VMEM((held, repeat, 2 * rows, 128), f32),
+            pltpu.VMEM((held, rows, 128), f32),
+            pltpu.VMEM((held, 2, repeat, rows, 128), f32),
+            pltpu.VMEM((held, rows, 128), f32),
+            dma((5,)), dma((len(constants),)),
             dma((held,)), dma((held,)), dma(()), dma(()),
             dma((held,)), dma((held,)), dma((held,)), dma((held,)),
         ],
         compiler_params=pltpu.CompilerParams(
-            collective_id=0, has_side_effects=True, vmem_limit_bytes=48 * 1024 * 1024
+            collective_id=0, has_side_effects=True, vmem_limit_bytes=64 * 1024 * 1024
         ),
         cost_estimate=pl.CostEstimate(
-            flops=12 * send.size * (rows + cols) * 4, bytes_accessed=moved, transcendentals=0
+            flops=48 * size * (rows + 128), bytes_accessed=8 * size, transcendentals=0
         ),
         name="exchange",
-    )(send, taps, *constants)
+    )(*inputs, *constants)
 
 
 def per_device(output_gate, input_gate, signal, cotangent, long_filter):
@@ -264,27 +329,13 @@
     chan_count = lax.axis_size("chan")
     channels, tok_local = signal.shape
     filters = long_filter.shape[0]
-    tokens = tok_local * seq_count
-    cols = 2 ** (int(math.log2(tokens)) // 2)
-    rows = tokens // cols
-    rows_dev = rows // seq_count
     spread = channels == filters and filters % (seq_count * chan_count) == 0
     repeat = chan_count if spread else 1
-    parts = seq_count * repeat
-    held = filters // parts
-
-    mixed = input_gate.astype(jnp.float32) * signal.astype(jnp.float32)
-    gated = cotangent.astype(jnp.float32) * output_gate.astype(jnp.float32)
-    send = jnp.stack([mixed, gated], axis=0).reshape(2, parts, held, rows_dev, cols)
-    send = send.transpose(1, 2, 0, 3, 4)
-    if spread:
-        block = held * seq_count
-        long_filter = lax.dynamic_slice_in_dim(
-            long_filter, lax.axis_index("chan") * block, block, axis=0
-        )
-    taps = long_filter.reshape(seq_count, held, rows_dev, cols)
-
-    results, kernel = exchange(send, taps, repeat, rows, cols)
+    held = filters // (seq_count * repeat)
+
+    results, kernel = exchange(
+        (output_gate, input_gate, signal, cotangent, long_filter), repeat, seq_count, held
+    )
 
     kernel = kernel.reshape(held * seq_count, tok_local)
     if not spread:

time: 66 us -> 62.6 us (0.948)
  the two profiles are of different devices: /device:TPU:0 before, /device:TPU:15 now
where the time goes in v3:
time: 62.6 us; the launch traced here: 62.4 us
  Pallas kernels  57.5 us (92%)
  local copies, waits for them, and re-layouts  3 us (5%)
  other arithmetic  1.19 us (2%)
  between operations  0.66 us (1%)
    pallas_call x1, Pallas kernels, exchange(): pl.pallas_call(functools.partial(exchange_kernel, repeat, seq_count, held...  57.5 us
    unnamed x7, local copies, waits for them, and re-layouts  1.66 us
    another operation x1, local copies, waits for them, and re-layouts, per_device(): response, grad_mixed = results.reshape(2, channels, tok_local)  1.34 us

profile of v3, /device:TPU:15, one launch (start us, length us, event | category | flops | bytes accessed | tf_op | source)
XLA Modules:
  0.0 62.4 jit_solution(17584011565809770931)
XLA Ops:
  0.6 57.5 %exchange.1 = (f32[2,64,16,128]{3,2,1,0:T(8,128)}, f32[16,16,128]{2,1,0:T(8,128)}) custom-call(bf16[64,2048]{1,0:T(8,128)(2,1)} %output_gate_ref.1, bf16[64,2048]{1,0:T(8,128)(2,1)} %input_gate_ref.1, bf16[64,2048]{1,0:T(8,128)(2,1)} %signal_ref.1, bf16[64,2048]{1,0:T(8,128)(2,1)} %cotangent_ref.1, f32[64,2048]{1,0:T(8,128)} %filter_ref.1, ...), custom_call_target="tpu_custom_call" | custom-call | flops 3221225472 | bytes 2097152 | tf_op jit(solution)/shard_map/exchange/pallas_call | solution.py:293
  58.2 1.6 %copy.21 = f32[2,8,16,128]{3,1,2,0:T(8,128)} copy(f32[2,8,16,128]{3,2,1,0:T(8,128)} %bitcast.22) | data formatting | bytes 262144
  59.8 0.0 copy-start
  59.8 0.0 copy-start.1
  59.8 0.0 copy-start.2
  59.8 1.3 %fusion.3 = (f32[1,64,16,128]{3,2,1,0:T(8,128)S(1)}, f32[1,64,16,128]{3,2,1,0:T(8,128)S(1)}) fusion(f32[2,64,16,128]{3,2,1,0:T(8,128)} %get-tuple-element.6), kind=kLoop, calls=%fused_computation.7 | loop fusion | bytes 2097152 | tf_op jit(solution)/shard_map/unstack | solution.py:343
  61.1 0.0 copy-done
  61.2 0.0 copy-done.1
  61.2 0.1 copy-done.2
  61.2 1.2 %fusion.1 = (bf16[64,2048]{1,0:T(8,128)(2,1)}, bf16[64,2048]{1,0:T(8,128)(2,1)}, bf16[64,2048]{1,0:T(8,128)(2,1)}) fusion(bf16[64,2048]{1,0:T(8,128)(2,1)S(1)} %copy-done, f32[8,8,16,128]{3,2,1,0:T(8,128)S(1)} %bitcast.19, bf16[64,2048]{1,0:T(8,128)(2,1)S(1)} %copy-done.1, f32[8,8,16,128]{3,2,1,0:T(8,128)S(1)} %bitcast.20, bf16[64,2048]{1,0:T(8,128)(2,1)S(1)} %copy-done.2), kind=kLoop, calls=%fused_computation.3 | loop fusion | flops 1179648 | bytes 2621440 | tf_op jit(solution)/shard_map/convert_element_type | solution.py:346
Async XLA Ops:
  59.8 1.4 %copy-start = (bf16[64,2048]{1,0:T(8,128)(2,1)S(1)}, bf16[64,2048]{1,0:T(8,128)(2,1)}, u32[]{:S(2)}) copy-start(bf16[64,2048]{1,0:T(8,128)(2,1)} %input_gate_ref.1) | copy-start | bytes 786436
  59.8 1.4 %copy-start.1 = (bf16[64,2048]{1,0:T(8,128)(2,1)S(1)}, bf16[64,2048]{1,0:T(8,128)(2,1)}, u32[]{:S(2)}) copy-start(bf16[64,2048]{1,0:T(8,128)(2,1)} %signal_ref.1) | copy-start | bytes 786436
  59.8 1.4 %copy-start.2 = (bf16[64,2048]{1,0:T(8,128)(2,1)S(1)}, bf16[64,2048]{1,0:T(8,128)(2,1)}, u32[]{:S(2)}) copy-start(bf16[64,2048]{1,0:T(8,128)(2,1)} %cotangent_ref.1) | copy-start | bytes 786436
